TPU v7x, 32 devices: a whole 2x2x4 slice. The times are simulated.
32 devices in a mesh: rep: 4 (over x, core), shard: 8 (over z, y).
Axes of the slice: x: 2, y: 2, z: 4, core: 2. Of those that a mesh axis runs over, the one named last changes fastest.
Arguments:
- hidden_in: bfloat16 [8192, 1280], P(('rep', 'shard')), may hold values from -6 to 6
- seg_ids: int32 [32, 256], P(('rep', 'shard')), may hold values from 0 to 1, as said below
- patch_rows: int32 [32, 256], P(('rep', 'shard')), may hold values from 0 to 31
- patch_cols: int32 [32, 256], P(('rep', 'shard')), may hold values from 0 to 31
- ln1_scale: bfloat16 [1280], P('shard'), may hold values from 0.5 to 1.5
- ln1_shift: bfloat16 [1280], P('shard'), may hold values from -1.5 to 1.5
- qkv_weight: bfloat16 [1280, 3840], P('shard'), may hold values from -0.15625 to 0.15625
- qkv_bias: bfloat16 [3840], P('shard'), may hold values from -1.5 to 1.5
- out_weight: bfloat16 [1280, 1280], P('shard'), may hold values from -1.25 to 1.25
- out_bias: bfloat16 [1280], P('shard'), may hold values from -1.5 to 1.5
- ln2_scale: bfloat16 [1280], P('shard'), may hold values from 0.5 to 1.5
- ln2_shift: bfloat16 [1280], P('shard'), may hold values from -1.5 to 1.5
- up_weight: bfloat16 [1280, 5120], P('shard'), may hold values from -0.15625 to 0.15625
- up_bias: bfloat16 [5120], P('shard'), may hold values from -1.5 to 1.5
- down_weight: bfloat16 [5120, 1280], P('shard'), may hold values from -0.078125 to 0.078125
- down_bias: bfloat16 [1280], P('shard'), may hold values from -1.5 to 1.5
- cotangent: bfloat16 [8192, 1280], P(('rep', 'shard')), may hold values from -6 to 6
Outputs:
- block_out: bfloat16 [8192, 1280], P(('rep', 'shard'))
- grad_in: bfloat16 [8192, 1280], P(('rep', 'shard'))
- grad_ln1_scale: float32 [1280], P('shard')
- grad_ln1_shift: float32 [1280], P('shard')
- grad_qkv_weight: float32 [1280, 3840], P('shard')
- grad_qkv_bias: float32 [3840], P('shard')
- grad_out_weight: float32 [1280, 1280], P('shard')
- grad_out_bias: float32 [1280], P('shard')
- grad_ln2_scale: float32 [1280], P('shard')
- grad_ln2_shift: float32 [1280], P('shard')
- grad_up_weight: float32 [1280, 5120], P('shard')
- grad_up_bias: float32 [5120], P('shard')
- grad_down_weight: float32 [5120, 1280], P('shard')
- grad_down_bias: float32 [1280], P('shard')
Inputs may be any that keep to these rules, and one draw needn't show every extreme that they name: `seg_ids`: each row numbers the images of one block of 256 consecutive patches in order, never falling. Every row holds exactly two images: one of exactly 192 patches and one of 64 patches, in either order.
All inputs are finite; a program needn't handle non-finite values.
Results may differ from a plain program's by a relative error of at most 0.013.
Values may be sent and summed in bfloat16 or wider, within the bound.
No kernel may reach another device: no remote copies, remote signals or barrier semaphores. Data moves between devices by JAX's collectives and lax.ppermute only.
A program may use at most 256 MiB of HBM per device.

v0:
```python
import jax
import jax.numpy as jnp
from jax import lax
from jax.sharding import PartitionSpec as P

HEADS = 16


EPSILON = 1e-06
GELU_SLOPE = 1.702


def norm_parts(values):
    center = values - jnp.mean(values, -1, keepdims=True)
    inverse = lax.rsqrt(jnp.mean(center * center, -1, keepdims=True) + EPSILON)
    return (center * inverse, inverse)


def norm_back(grad_normed, unit, inverse, scale):
    scaled = grad_normed * scale
    return inverse * (
        scaled
        - jnp.mean(scaled, -1, keepdims=True)
        - unit * jnp.mean(scaled * unit, -1, keepdims=True)
    )


def rotate_half(values):
    middle = values.shape[-1] // 2
    return jnp.concatenate([-values[..., middle:], values[..., :middle]], -1)


def rotary(rows, columns, head_dim):
    quarter = head_dim // 4
    inverse = 10000.0 ** (-4.0 * jnp.arange(quarter, dtype=jnp.float32) / head_dim)
    row_angles = rows.astype(jnp.float32)[:, None] * inverse
    column_angles = columns.astype(jnp.float32)[:, None] * inverse
    halfway = jnp.concatenate([row_angles, column_angles], -1)
    angles = jnp.concatenate([halfway, halfway], -1)
    return (jnp.cos(angles)[:, None, :], jnp.sin(angles)[:, None, :])


def outer(left, right):
    return lax.dot_general(
        left, right, (((0,), (0,)), ((), ())), preferred_element_type=jnp.float32
    )


def times_transposed(left, right):
    return lax.dot_general(
        left, right, (((1,), (1,)), ((), ())), preferred_element_type=jnp.float32
    )


def on_device(
    hidden_in,
    seg_ids,
    patch_rows,
    patch_cols,
    ln1_scale,
    ln1_shift,
    qkv_weight,
    qkv_bias,
    out_weight,
    out_bias,
    ln2_scale,
    ln2_shift,
    up_weight,
    up_bias,
    down_weight,
    down_bias,
    cotangent,
):
    length, width = hidden_in.shape
    head_dim = width // HEADS
    scale_factor = head_dim ** (-0.5)
    attn_full = (
        lax.all_gather(ln1_scale, "shard", axis=0, tiled=True),
        lax.all_gather(ln1_shift, "shard", axis=0, tiled=True),
        lax.all_gather(qkv_weight, "shard", axis=0, tiled=True),
        lax.all_gather(qkv_bias, "shard", axis=0, tiled=True),
        lax.all_gather(out_weight, "shard", axis=0, tiled=True),
        lax.all_gather(out_bias, "shard", axis=0, tiled=True),
    )
    mlp_full = (
        lax.all_gather(ln2_scale, "shard", axis=0, tiled=True),
        lax.all_gather(ln2_shift, "shard", axis=0, tiled=True),
        lax.all_gather(up_weight, "shard", axis=0, tiled=True),
        lax.all_gather(up_bias, "shard", axis=0, tiled=True),
        lax.all_gather(down_weight, "shard", axis=0, tiled=True),
        lax.all_gather(down_bias, "shard", axis=0, tiled=True),
    )
    gain_one, shift_one, qkv_full, qkv_offset, out_full, out_offset = attn_full
    gain_two, shift_two, up_full, up_offset, down_full, down_offset = mlp_full
    inputs = hidden_in.astype(jnp.float32)
    unit_one, inverse_one = norm_parts(inputs)
    normed_one = (unit_one * gain_one.astype(jnp.float32) + shift_one.astype(jnp.float32)).astype(
        jnp.bfloat16
    )
    projected = jnp.dot(
        normed_one, qkv_full, preferred_element_type=jnp.float32
    ) + qkv_offset.astype(jnp.float32)
    projected = projected.reshape(length, 3, HEADS, head_dim)
    cosine, sine = rotary(patch_rows[0], patch_cols[0], head_dim)
    queries = (projected[:, 0] * cosine + rotate_half(projected[:, 0]) * sine).astype(jnp.bfloat16)
    keys_rot = (projected[:, 1] * cosine + rotate_half(projected[:, 1]) * sine).astype(jnp.bfloat16)
    values_low = projected[:, 2].astype(jnp.bfloat16)
    images = seg_ids[0]
    same = (images[:, None] == images[None, :])[None]

    def scores_of():
        raw = (
            jnp.einsum("thd,shd->hts", queries, keys_rot, preferred_element_type=jnp.float32)
            * scale_factor
        )
        return jnp.where(same, raw, -1e30)

    scores = scores_of()
    row_max = jnp.max(scores, -1, keepdims=True)
    expo = jnp.exp(scores - row_max)
    total = jnp.sum(expo, -1, keepdims=True)
    probs = expo / total
    log_total = row_max + jnp.log(total)
    mixed = jnp.einsum(
        "hts,shd->thd", probs.astype(jnp.bfloat16), values_low, preferred_element_type=jnp.float32
    )
    mixed = mixed.reshape(length, width).astype(jnp.bfloat16)
    middle = (
        inputs
        + jnp.dot(mixed, out_full, preferred_element_type=jnp.float32)
        + out_offset.astype(jnp.float32)
    )
    unit_two, inverse_two = norm_parts(middle)
    normed_two = (unit_two * gain_two.astype(jnp.float32) + shift_two.astype(jnp.float32)).astype(
        jnp.bfloat16
    )
    upward = jnp.dot(normed_two, up_full, preferred_element_type=jnp.float32) + up_offset.astype(
        jnp.float32
    )
    sigma = jax.nn.sigmoid(GELU_SLOPE * upward)
    activated = (upward * sigma).astype(jnp.bfloat16)
    output = (
        middle
        + jnp.dot(activated, down_full, preferred_element_type=jnp.float32)
        + down_offset.astype(jnp.float32)
    )
    mlp_back = (
        lax.all_gather(ln2_scale, "shard", axis=0, tiled=True),
        lax.all_gather(ln2_shift, "shard", axis=0, tiled=True),
        lax.all_gather(up_weight, "shard", axis=0, tiled=True),
        lax.all_gather(up_bias, "shard", axis=0, tiled=True),
        lax.all_gather(down_weight, "shard", axis=0, tiled=True),
        lax.all_gather(down_bias, "shard", axis=0, tiled=True),
    )
    gain_two_b, shift_two_b, up_back, up_offset_b, down_back, down_offset_b = mlp_back
    grad_out = cotangent.astype(jnp.float32)
    grad_down = outer(activated, cotangent)
    grad_down_bias = jnp.sum(grad_out, 0)
    grad_act = times_transposed(cotangent, down_back)
    grad_up_low = (grad_act * (sigma + GELU_SLOPE * upward * sigma * (1.0 - sigma))).astype(
        jnp.bfloat16
    )
    grad_up = outer(normed_two, grad_up_low)
    grad_up_bias = jnp.sum(grad_up_low.astype(jnp.float32), 0)
    grad_normed_two = times_transposed(grad_up_low, up_back)
    grad_gain_two = jnp.sum(grad_normed_two * unit_two, 0)
    grad_shift_two = jnp.sum(grad_normed_two, 0)
    grad_middle = grad_out + norm_back(
        grad_normed_two, unit_two, inverse_two, gain_two_b.astype(jnp.float32)
    )
    attn_back = (
        lax.all_gather(ln1_scale, "shard", axis=0, tiled=True),
        lax.all_gather(ln1_shift, "shard", axis=0, tiled=True),
        lax.all_gather(qkv_weight, "shard", axis=0, tiled=True),
        lax.all_gather(qkv_bias, "shard", axis=0, tiled=True),
        lax.all_gather(out_weight, "shard", axis=0, tiled=True),
        lax.all_gather(out_bias, "shard", axis=0, tiled=True),
    )
    gain_one_b, shift_one_b, qkv_back, qkv_offset_b, out_back, out_offset_b = attn_back
    grad_branch = grad_middle.astype(jnp.bfloat16)
    grad_out_w = outer(mixed, grad_branch)
    grad_out_b = jnp.sum(grad_branch.astype(jnp.float32), 0)
    grad_mixed = (
        times_transposed(grad_branch, out_back)
        .astype(jnp.bfloat16)
        .reshape(length, HEADS, head_dim)
    )
    probs_again = jnp.exp(scores_of() - log_total)
    probs_low = probs_again.astype(jnp.bfloat16)
    grad_probs = jnp.einsum(
        "thd,shd->hts", grad_mixed, values_low, preferred_element_type=jnp.float32
    )
    grad_values = jnp.einsum(
        "hts,thd->shd", probs_low, grad_mixed, preferred_element_type=jnp.float32
    )
    grad_scores = probs_again * (grad_probs - jnp.sum(probs_again * grad_probs, -1, keepdims=True))
    grad_scores_low = grad_scores.astype(jnp.bfloat16)
    grad_queries = (
        jnp.einsum("hts,shd->thd", grad_scores_low, keys_rot, preferred_element_type=jnp.float32)
        * scale_factor
    )
    grad_keys = (
        jnp.einsum("hts,thd->shd", grad_scores_low, queries, preferred_element_type=jnp.float32)
        * scale_factor
    )
    grad_queries = grad_queries * cosine - rotate_half(grad_queries * sine)
    grad_keys = grad_keys * cosine - rotate_half(grad_keys * sine)
    grad_projected = (
        jnp.stack([grad_queries, grad_keys, grad_values], 1)
        .reshape(length, 3 * width)
        .astype(jnp.bfloat16)
    )
    grad_qkv = outer(normed_one, grad_projected)
    grad_qkv_bias = jnp.sum(grad_projected.astype(jnp.float32), 0)
    grad_normed_one = times_transposed(grad_projected, qkv_back)
    grad_gain_one = jnp.sum(grad_normed_one * unit_one, 0)
    grad_shift_one = jnp.sum(grad_normed_one, 0)
    grad_inputs = grad_middle + norm_back(
        grad_normed_one, unit_one, inverse_one, gain_one_b.astype(jnp.float32)
    )
    pieces = (
        lax.psum_scatter(grad_gain_one, "shard", scatter_dimension=0, tiled=True),
        lax.psum_scatter(grad_shift_one, "shard", scatter_dimension=0, tiled=True),
        lax.psum_scatter(grad_qkv, "shard", scatter_dimension=0, tiled=True),
        lax.psum_scatter(grad_qkv_bias, "shard", scatter_dimension=0, tiled=True),
        lax.psum_scatter(grad_out_w, "shard", scatter_dimension=0, tiled=True),
        lax.psum_scatter(grad_out_b, "shard", scatter_dimension=0, tiled=True),
        lax.psum_scatter(grad_gain_two, "shard", scatter_dimension=0, tiled=True),
        lax.psum_scatter(grad_shift_two, "shard", scatter_dimension=0, tiled=True),
        lax.psum_scatter(grad_up, "shard", scatter_dimension=0, tiled=True),
        lax.psum_scatter(grad_up_bias, "shard", scatter_dimension=0, tiled=True),
        lax.psum_scatter(grad_down, "shard", scatter_dimension=0, tiled=True),
        lax.psum_scatter(grad_down_bias, "shard", scatter_dimension=0, tiled=True),
    )
    flat_grads = jnp.concatenate([piece.reshape(-1) for piece in pieces])
    summed_share = lax.psum_scatter(flat_grads, "rep", scatter_dimension=0, tiled=True)
    summed_whole = lax.all_gather(summed_share, "rep", axis=0, tiled=True)
    totals = []
    offset_now = 0
    for piece in pieces:
        sized = piece.size
        totals.append(summed_whole[offset_now : offset_now + sized].reshape(piece.shape))
        offset_now = offset_now + sized
    return (
        output.astype(jnp.bfloat16),
        grad_inputs.astype(jnp.bfloat16),
        totals[0],
        totals[1],
        totals[2],
        totals[3],
        totals[4],
        totals[5],
        totals[6],
        totals[7],
        totals[8],
        totals[9],
        totals[10],
        totals[11],
    )


def solution(mesh):
    in_specs = (
        P(("rep", "shard"), None),
        P(("rep", "shard"), None),
        P(("rep", "shard"), None),
        P(("rep", "shard"), None),
        P("shard"),
        P("shard"),
        P("shard", None),
        P("shard"),
        P("shard", None),
        P("shard"),
        P("shard"),
        P("shard"),
        P("shard", None),
        P("shard"),
        P("shard", None),
        P("shard"),
        P(("rep", "shard"), None),
    )
    out_specs = (
        P(("rep", "shard"), None),
        P(("rep", "shard"), None),
        P("shard"),
        P("shard"),
        P("shard", None),
        P("shard"),
        P("shard", None),
        P("shard"),
        P("shard"),
        P("shard"),
        P("shard", None),
        P("shard"),
        P("shard", None),
        P("shard"),
    )
    return jax.shard_map(
        on_device, mesh=mesh, in_specs=in_specs, out_specs=out_specs, check_vma=False
    )
```

profile of v0, /device:TPU:0, one launch (start us, length us, event | category | flops | bytes accessed | tf_op | source)
XLA Modules:
  0.0 2509.9 jit_solution(15608723329803953300)
XLA Ops:
  14.0 40.5 %all-reduce.18 = (bf16[3840]{0:T(1024)(128)(2,1)S(1)}, bf16[1280]{0:T(1024)(128)(2,1)S(1)}, bf16[1280]{0:T(1024)(128)(2,1)S(1)}, bf16[1280]{0:T(1024)(128)(2,1)S...) all-reduce(bf16[3840]{0:T(1024)(128)(2,1)S(1)} %dynamic-update-slic, ...), channel_id=1, replica_groups=mesh['rep'=4,'shard'=8] {'shard'}, use_global_device_ids=true, to_apply=%add.2 | all-reduce | flops 11520 | bytes 46080
  54.5 30.6 %all-gather = bf16[8,1,640]{2,1,0:T(2,128)(2,1)S(1)} all-gather(bf16[1,1,640]{2,1,0:T(2,128)(2,1)S(1)} %reshape.302), channel_id=1, replica_groups=mesh['rep'=4,'shard'=8] {'shard'}, dimensions={0}, use_global_device_ids=true | all-gather | bytes 11520 | tf_op jit(solution)/shard_map/all_gather | solution.py:89
  86.2 70.2 %all-gather.6.cloned.1.call-done = bf16[1280,3840]{1,0:T(8,128)(2,1)} async-done(((bf16[160,3840]{1,0:T(8,128)(2,1)}), bf16[1280,3840]{1,0:T(8,128)(2,1)}) %all-gather.6.cloned.1.call-update) | async-done | bytes 9830416 | tf_op jit(solution)/shard_map/all_gather | solution.py:80
  156.4 8.7 convolution_add_fusion.1
  179.4 39.3 %all-gather.8.cloned.1.call-done = bf16[1280,1280]{1,0:T(8,128)(2,1)} async-done(((bf16[160,1280]{1,0:T(8,128)(2,1)}), bf16[1280,1280]{1,0:T(8,128)(2,1)}) %all-gather.8.cloned.1.call-update) | async-done | bytes 3276816 | tf_op jit(solution)/shard_map/all_gather | solution.py:82
  222.1 180.2 %all-gather.10.cloned.1.call-done = bf16[1280,5120]{1,0:T(8,128)(2,1)} async-done(((bf16[160,5120]{1,0:T(8,128)(2,1)}), bf16[1280,5120]{1,0:T(8,128)(2,1)}) %all-gather.10.cloned.1.call-update) | async-done | bytes 13107216 | tf_op jit(solution)/shard_map/all_gather | solution.py:88
  402.4 10.3 convolution_add_fusion
  412.7 172.8 %all-gather.12.cloned.1.call-done = bf16[5120,1280]{1,0:T(8,128)(2,1)} async-done(((bf16[640,1280]{1,0:T(8,128)(2,1)}), bf16[5120,1280]{1,0:T(8,128)(2,1)}) %all-gather.12.cloned.1.call-update) | async-done | bytes 13107216 | tf_op jit(solution)/shard_map/all_gather | solution.py:90
  585.4 16.0 convert_reduce_fusion
  601.4 9.3 multiply_reduce_fusion.1
  628.0 9.0 fusion.27
  642.0 10.1 fusion.44
  652.2 12.5 fusion.47
  664.7 16.1 fusion.48
  682.8 23.1 all-reduce.27.cloned.1.call-done
  712.0 119.1 %reduce-scatter.7.cloned.1.call-done = f32[160,1280]{1,0:T(8,128)} async-done(((f32[1280,1280]{1,0:T(8,128)}), f32[160,1280]{1,0:T(8,128)}) %reduce-scatter.7.cloned.1.call-update) | async-done | bytes 819216 | tf_op jit(solution)/shard_map/reduce_scatter | solution.py:226
  833.2 326.1 %reduce-scatter.5.cloned.1.call-done = f32[160,3840]{1,0:T(8,128)} async-done(((f32[1280,3840]{1,0:T(8,128)}), f32[160,3840]{1,0:T(8,128)}) %reduce-scatter.5.cloned.1.call-update) | async-done | bytes 2457616 | tf_op jit(solution)/shard_map/reduce_scatter | solution.py:224
  1162.6 418.7 %reduce-scatter.9.cloned.1.call-done = f32[160,5120]{1,0:T(8,128)} async-done(((f32[1280,5120]{1,0:T(8,128)}), f32[160,5120]{1,0:T(8,128)}) %reduce-scatter.9.cloned.1.call-update) | async-done | bytes 3276816 | tf_op jit(solution)/shard_map/reduce_scatter | solution.py:230
  1585.5 417.3 %reduce-scatter.11.cloned.1.call-done = f32[640,1280]{1,0:T(8,128)} async-done(((f32[5120,1280]{1,0:T(8,128)}), f32[640,1280]{1,0:T(8,128)}) %reduce-scatter.11.cloned.1.call-update) | async-done | bytes 3276816 | tf_op jit(solution)/shard_map/reduce_scatter | solution.py:232
  2007.2 87.4 %concatenate.33 = f32[2459680]{0:T(1024)} concatenate(f32[160]{0:T(256)S(1)} %dynamic-slice.9, f32[160]{0:T(256)S(1)} %dynamic-slice.11, f32[614400]{0:T(1024)} %reshape.270, f32[480]{0:T(512)S(1)} %dynamic-slice.13, f32[204800]{0:T(1024)} %reshape.271, f32[160]{0:T(256)S(1)} %dynamic-slice.15, f32[160]{0:T(256)S(1)} %dynamic-slice.17, f32[160]{0:T(256)S(1)} %dynamic-slice.19, ...), dimensions={0} | concatenate | bytes 19677440 | tf_op jit(solution)/shard_map/concatenate | solution.py:235
  2096.0 174.8 %all-reduce.25.cloned.1.call-done = f32[2459680]{0:T(1024)} async-done(((f32[2459680]{0:T(1024)}), f32[2459680]{0:T(1024)}) %all-reduce.25.cloned.1.call-update) | async-done | bytes 9838736
  2278.9 21.8 dynamic-update-slice.7
  2304.0 12.3 fusion.5
  2316.3 161.5 %all-reduce.23.cloned.1.call-done = f32[2459680]{0:T(1024)} async-done(((f32[2459680]{0:T(1024)}), f32[2459680]{0:T(1024)}) %all-reduce.23.cloned.1.call-update) | async-done | bytes 9838736
  (166 shorter events, 103.2 us)
Async XLA Ops:
  7.2 149.2 %all-gather.6.cloned.1.call-start = ((), (), s32[]{:S(2)}) async-start(), calls=%async_computation.4 | async-start | bytes 11059200 | tf_op jit(solution)/shard_map/all_gather | solution.py:80
  8.0 4.2 copy-start.16
  8.0 4.2 copy-start.21
  8.0 4.5 copy-start.22
  8.0 4.7 copy-start.23
  8.0 5.0 copy-start.24
  8.0 5.2 copy-start.25
  8.0 5.4 copy-start.26
  8.0 5.7 copy-start.19
  8.0 210.7 %all-gather.8.cloned.1.call-start = ((), (), s32[]{:S(2)}) async-start(), calls=%async_computation.5 | async-start | bytes 3686400 | tf_op jit(solution)/shard_map/all_gather | solution.py:82
  8.8 76.7 %copy-start.3 = (bf16[256,1280]{1,0:T(8,128)(2,1)S(1)}, bf16[256,1280]{1,0:T(8,128)(2,1)}, u32[]{:S(2)}) copy-start(bf16[256,1280]{1,0:T(8,128)(2,1)} %param.17) | copy-start | bytes 1966084
  8.8 393.5 %all-gather.10.cloned.1.call-start = ((), (), s32[]{:S(2)}) async-start(), calls=%async_computation.6 | async-start | bytes 14745600 | tf_op jit(solution)/shard_map/all_gather | solution.py:88
  9.5 76.5 %copy-start.13 = (s32[1,256]{1,0:T(1,128)S(1)}, s32[1,256]{1,0:T(1,128)}, u32[]{:S(2)}) copy-start(s32[1,256]{1,0:T(1,128)} %param.18) | copy-start | bytes 3076
  9.5 575.9 %all-gather.12.cloned.1.call-start = ((), (), s32[]{:S(2)}) async-start(), calls=%async_computation.7 | async-start | bytes 14745600 | tf_op jit(solution)/shard_map/all_gather | solution.py:90
  10.1 695.7 %all-reduce.27.cloned.1.call-start = ((), (), s32[]{:S(2)}) async-start(), calls=%async_computation.14 | async-start | bytes 172032
  179.4 42.4 %copy-start.11 = (bf16[16,80,256]{2,1,0:T(8,128)(2,1)}, bf16[16,80,256]{2,1,0:T(8,128)(2,1)S(1)}, u32[]{:S(2)}) copy-start(bf16[16,80,256]{2,1,0:T(8,128)(2,1)S(1)} %fusion.19) | copy-start | bytes 1966084
  402.3 183.1 %copy-start.9 = (bf16[256,1280]{1,0:T(8,128)(2,1)S(1)}, bf16[256,1280]{1,0:T(8,128)(2,1)}, u32[]{:S(2)}) copy-start(bf16[256,1280]{1,0:T(8,128)(2,1)} %param.33) | copy-start | bytes 1966084
  601.4 9.3 copy-start.10
  637.1 194.0 %reduce-scatter.7.cloned.1.call-start = ((), (), s32[]{:S(2)}) async-start(), calls=%async_computation.9 | async-start | bytes 7372800 | tf_op jit(solution)/shard_map/reduce_scatter | solution.py:226
  642.0 517.4 %reduce-scatter.5.cloned.1.call-start = ((), (), s32[]{:S(2)}) async-start(), calls=%async_computation.8 | async-start | bytes 22118400 | tf_op jit(solution)/shard_map/reduce_scatter | solution.py:224
  652.1 929.1 %reduce-scatter.9.cloned.1.call-start = ((), (), s32[]{:S(2)}) async-start(), calls=%async_computation.10 | async-start | bytes 29491200 | tf_op jit(solution)/shard_map/reduce_scatter | solution.py:230
  664.7 1338.1 %reduce-scatter.11.cloned.1.call-start = ((), (), s32[]{:S(2)}) async-start(), calls=%async_computation.11 | async-start | bytes 29491200 | tf_op jit(solution)/shard_map/reduce_scatter | solution.py:232
  680.8 1590.0 %all-reduce.25.cloned.1.call-start = ((), (), s32[]{:S(2)}) async-start(), calls=%async_computation.13 | async-start | bytes 19685376
  2094.6 383.2 %all-reduce.23.cloned.1.call-start = ((), (), s32[]{:S(2)}) async-start(), calls=%async_computation.12 | async-start | bytes 19685376
  (14 other events, 28.2 us)
Sparse Core Ops, SparseCore 0:
  10.2 146.1 all-gather.5
  158.5 60.1 all-gather.7
  220.9 181.3 all-gather.9
  404.4 180.9 all-gather.11
  637.2 68.6 all-reduce.26
  709.3 121.7 reduce-scatter.6
  835.5 323.7 reduce-scatter.4
  1163.8 417.4 reduce-scatter.8
  1585.2 417.5 reduce-scatter.10
  2094.8 176.0 all-reduce.24
  2300.8 176.9 all-reduce.22
where the time goes:
time: 2520 us; the launch traced here: 2510 us
  waiting for transfers between devices  2110 us (84%)
  local copies, waits for them, and re-layouts  181 us (7%)
  matrix products  122 us (5%)
  blocking collectives  71.1 us (3%)
    reduce_scatter x1, waiting for transfers between devices, on_device(): lax.psum_scatter(grad_up, 'shard', scatter_dimension=0, tiled=True)  419 us
    reduce_scatter x1, waiting for transfers between devices, on_device(): lax.psum_scatter(grad_down, 'shard', scatter_dimension=0, tiled=True)  417 us
    unnamed x14, waiting for transfers between devices  362 us
    reduce_scatter x1, waiting for transfers between devices, on_device(): lax.psum_scatter(grad_qkv, 'shard', scatter_dimension=0, tiled=True)  326 us
    all_gather x1, waiting for transfers between devices, on_device(): lax.all_gather(up_weight, 'shard', axis=0, tiled=True)  180 us
    all_gather x1, waiting for transfers between devices, on_device(): lax.all_gather(down_weight, 'shard', axis=0, tiled=True)  173 us
    reduce_scatter x1, waiting for transfers between devices, on_device(): lax.psum_scatter(grad_out_w, 'shard', scatter_dimension=0, tiled=True)  119 us
    concatenate x1, local copies, waits for them, and re-layouts, on_device(): flat_grads = jnp.concatenate([piece.reshape(-1) for piece in pieces])  87.4 us
  transfers between devices with their start and end apart: 11, of which 11 were waited for; matrix products, arithmetic and copies ran while one was open for 4% of the time, Pallas kernels for 0%

commit v1 on v0

v1 whole, which is shorter than its diff:
```python
import jax
import jax.numpy as jnp
import numpy as np
from jax import lax
from jax.experimental import pallas as pl
from jax.experimental.pallas import tpu as pltpu
from jax.sharding import PartitionSpec as P

HEADS = 16
EPSILON = 1e-06
GELU_SLOPE = 1.702
LANES = 128
MASKED = -1e30

CORE_PAIRS = [(0, 1), (1, 0), (2, 3), (3, 2)]
X_PAIRS = [(0, 2), (2, 0), (1, 3), (3, 1)]
RING = (0, 2, 4, 6, 7, 5, 3, 1)
RING_AT = tuple(RING.index(i) for i in range(8))
RIGHT = [(RING[i], RING[(i + 1) % 8]) for i in range(8)]
LEFT = [(RING[i], RING[(i - 1) % 8]) for i in range(8)]

F32 = jnp.float32
BF16 = jnp.bfloat16


def norm_parts(values):
    center = values - jnp.mean(values, -1, keepdims=True)
    inverse = lax.rsqrt(jnp.mean(center * center, -1, keepdims=True) + EPSILON)
    return (center * inverse, inverse)


def norm_back(grad_normed, unit, inverse, scale):
    scaled = grad_normed * scale
    return inverse * (
        scaled
        - jnp.mean(scaled, -1, keepdims=True)
        - unit * jnp.mean(scaled * unit, -1, keepdims=True)
    )


def outer(left, right):
    return lax.dot_general(left, right, (((0,), (0,)), ((), ())), preferred_element_type=F32)


def times_transposed(left, right):
    return lax.dot_general(left, right, (((1,), (1,)), ((), ())), preferred_element_type=F32)


def times(left, right):
    return jnp.dot(left, right, preferred_element_type=F32)


def to_core(value):
    return lax.ppermute(value, "rep", CORE_PAIRS)


def to_x(value):
    return lax.ppermute(value, "rep", X_PAIRS)


def gather_rep(value):
    near, far = to_core(value), to_x(value)
    return [value, near, far, to_core(far)]


def reduce_pair(parts):
    low = parts.astype(BF16)
    arrived = to_core(jnp.stack([low[1], low[3]]))
    return (jnp.stack([low[0], low[2]]).astype(F32) + arrived.astype(F32)).astype(BF16)


def scatter_rep(parts):
    pair = reduce_pair(parts)
    return pair[0].astype(F32) + to_x(pair[1]).astype(F32)


def sum_rep(parts):
    pair = reduce_pair(parts)
    arrived = to_x(pair)
    total = (pair.astype(F32) + arrived[::-1].astype(F32)).astype(BF16)
    near = to_core(total)
    return jnp.stack([total[0], near[0], total[1], near[1]])


def by_owner(slots, me):
    core, far = me % 2 == 1, me // 2 == 1
    a, b, c, d = slots
    a, b, c, d = (
        jnp.where(core, b, a),
        jnp.where(core, a, b),
        jnp.where(core, d, c),
        jnp.where(core, c, d),
    )
    return [jnp.where(far, c, a), jnp.where(far, d, b), jnp.where(far, a, c), jnp.where(far, b, d)]


def ring_slot(position, step):
    return jnp.asarray(RING, jnp.int32)[(position + step) % 8]


def gather_shards(pieces, shards):
    if shards != 8:
        return [lax.all_gather(piece, "shard", axis=0) for piece in pieces]
    position = jnp.asarray(RING_AT, jnp.int32)[lax.axis_index("shard")]
    outs = []
    for number, piece in enumerate(pieces):
        rights = 4 if number % 2 == 0 else 3
        whole = jnp.zeros((8,) + piece.shape, piece.dtype)
        right = left = piece
        whole = lax.dynamic_update_slice(whole, piece[None], (ring_slot(position, 0), 0, 0))
        for step in range(1, 5):
            if step <= rights:
                right = lax.ppermute(right, "shard", RIGHT)
                whole = lax.dynamic_update_slice(
                    whole, right[None], (ring_slot(position, 8 - step), 0, 0)
                )
            if step <= 7 - rights:
                left = lax.ppermute(left, "shard", LEFT)
                whole = lax.dynamic_update_slice(
                    whole, left[None], (ring_slot(position, step), 0, 0)
                )
        outs.append(whole)
    return outs


def scatter_shards(whole, shards, rights):
    if shards != 8:
        return lax.psum_scatter(whole, "shard", scatter_dimension=0, tiled=False)
    position = jnp.asarray(RING_AT, jnp.int32)[lax.axis_index("shard")]

    def own(step):
        return lax.dynamic_index_in_dim(whole, ring_slot(position, step), 0, False)

    def plus(one, other):
        return (one.astype(F32) + other.astype(F32)).astype(whole.dtype)

    right = left = None
    for step in range(4, 0, -1):
        if step <= rights:
            term = own(step)
            right = lax.ppermute(term if right is None else plus(right, term), "shard", RIGHT)
        if step <= 7 - rights:
            term = own(8 - step)
            left = lax.ppermute(term if left is None else plus(left, term), "shard", LEFT)
    return (right.astype(F32) + left.astype(F32) + own(0).astype(F32)).astype(whole.dtype)


def window(values, start, size):
    part = values[:, start : start + size]
    return jnp.concatenate([part, jnp.zeros((part.shape[0], LANES - size), part.dtype)], 1)


def turned(values, half, lane):
    return jnp.where(
        lane < half,
        pltpu.roll(values, LANES - half, 1),
        pltpu.roll(values, half, 1),
    )


def attend_kernel(
    heads, size, x_ref, gain_ref, shift_ref, w_ref, bias_ref, cos_ref, sin_ref, row_ref, col_ref,
    normed_ref, qkv_ref, lse_ref, out_ref,
):
    unit, _ = norm_parts(x_ref[...].astype(F32))
    normed = (unit * gain_ref[...] + shift_ref[...]).astype(BF16)
    normed_ref[...] = normed
    projected = times(normed, w_ref[...]) + bias_ref[...]
    cosine, sine = cos_ref[...], sin_ref[...]
    rows = projected.shape[0]
    lane = lax.broadcasted_iota(jnp.int32, (rows, LANES), 1)
    same = col_ref[...] == row_ref[0]
    scale = size**-0.5
    half = size // 2
    outs = []
    lses = jnp.zeros((rows, LANES), F32)
    for head in range(heads):
        query, key, value = (
            window(projected, (part * heads + head) * size, size) for part in range(3)
        )
        query = (query * cosine + turned(query, half, lane) * sine).astype(BF16)
        key = (key * cosine + turned(key, half, lane) * sine).astype(BF16)
        value = value.astype(BF16)
        for part, kept in enumerate((query, key, value)):
            at = (part * heads + head) * LANES
            qkv_ref[:, at : at + LANES] = kept
        scores = jnp.where(same, times_transposed(query, key) * scale, MASKED)
        most = jnp.max(scores, -1, keepdims=True)
        expo = jnp.exp(scores - most)
        total = jnp.sum(expo, -1, keepdims=True)
        probs = (expo * (1.0 / total)).astype(BF16)
        outs.append(times(probs, value)[:, :size])
        lses = jnp.where(lane == head, most + jnp.log(total), lses)
    lse_ref[...] = lses
    out_ref[...] = jnp.concatenate(outs, 1).astype(BF16)


def attend(x, gain, shift, weight, bias, cosine, sine, seg_rows, seg_cols, heads, size):
    tokens, width = x.shape
    length = seg_rows.shape[-1]
    part = heads * size
    by_block = lambda columns: pl.BlockSpec((length, columns), lambda i: (i, 0))
    fixed = lambda array: pl.BlockSpec(array.shape, lambda i: (0,) * array.ndim)
    return pl.pallas_call(
        lambda *refs: attend_kernel(heads, size, *refs),
        grid=(tokens // length,),
        in_specs=[
            by_block(width),
            fixed(gain),
            fixed(shift),
            fixed(weight),
            fixed(bias),
            by_block(LANES),
            by_block(LANES),
            pl.BlockSpec((1, 1, length), lambda i: (i, 0, 0)),
            by_block(1),
        ],
        out_specs=[by_block(width), by_block(3 * heads * LANES), by_block(LANES), by_block(part)],
        out_shape=[
            jax.ShapeDtypeStruct((tokens, width), BF16),
            jax.ShapeDtypeStruct((tokens, 3 * heads * LANES), BF16),
            jax.ShapeDtypeStruct((tokens, LANES), F32),
            jax.ShapeDtypeStruct((tokens, part), BF16),
        ],
        compiler_params=pltpu.CompilerParams(vmem_limit_bytes=48 * 1024 * 1024),
        cost_estimate=pl.CostEstimate(
            flops=2 * tokens * width * 3 * part + 4 * tokens * length * part,
            bytes_accessed=4 * tokens * width + weight.size * 2 + tokens * 3 * heads * LANES * 2,
            transcendentals=tokens * length * heads,
        ),
    )(x, gain, shift, weight, bias, cosine, sine, seg_rows, seg_cols)


def attend_back_kernel(
    heads, size, db_ref, wo_ref, qkv_ref, lse_ref, cos_ref, sin_ref, row_ref, col_ref, w_ref,
    x_ref, grad_ref, dn_ref, sum_ref, gain_ref, shift_ref,
):
    mixed = times_transposed(db_ref[...], wo_ref[...])
    cosine, sine = cos_ref[...], sin_ref[...]
    rows = mixed.shape[0]
    lane = lax.broadcasted_iota(jnp.int32, (rows, LANES), 1)
    same = col_ref[...] == row_ref[0]
    scale = size**-0.5
    half = size // 2
    lses = lse_ref[...]
    grads = [None] * (3 * heads)
    for head in range(heads):
        query, key, value = (
            qkv_ref[:, (part * heads + head) * LANES : (part * heads + head + 1) * LANES]
            for part in range(3)
        )
        lse = jnp.sum(jnp.where(lane == head, lses, 0.0), -1, keepdims=True)
        scores = jnp.where(same, times_transposed(query, key) * scale, MASKED)
        probs = jnp.exp(scores - lse)
        grad_mixed = window(mixed, head * size, size).astype(BF16)
        grad_probs = times_transposed(grad_mixed, value)
        grad_value = outer(probs.astype(BF16), grad_mixed)
        inner = jnp.sum(probs * grad_probs, -1, keepdims=True)
        low = (probs * (grad_probs - inner)).astype(BF16)
        grad_query = times(low, key) * scale
        grad_key = outer(low, query) * scale
        grad_query = grad_query * cosine + turned(grad_query * sine, half, lane)
        grad_key = grad_key * cosine + turned(grad_key * sine, half, lane)
        grads[head] = grad_query[:, :size]
        grads[heads + head] = grad_key[:, :size]
        grads[2 * heads + head] = grad_value[:, :size]
    grad = jnp.concatenate(grads, 1).astype(BF16)
    grad_ref[...] = grad
    grad_normed = times_transposed(grad, w_ref[...])
    dn_ref[...] = grad_normed.astype(BF16)
    unit, _ = norm_parts(x_ref[...].astype(F32))

    @pl.when(pl.program_id(0) == 0)
    def _():
        sum_ref[...] = jnp.zeros_like(sum_ref)
        gain_ref[...] = jnp.zeros_like(gain_ref)
        shift_ref[...] = jnp.zeros_like(shift_ref)

    sum_ref[...] += jnp.sum(grad.astype(F32), 0, keepdims=True)
    gain_ref[...] += jnp.sum(grad_normed * unit, 0, keepdims=True)
    shift_ref[...] += jnp.sum(grad_normed, 0, keepdims=True)


def attend_back(db, w_out, qkv, lse, cosine, sine, seg_rows, seg_cols, weight, x, heads, size):
    tokens, width = x.shape
    length = seg_rows.shape[-1]
    part = heads * size
    by_block = lambda columns: pl.BlockSpec((length, columns), lambda i: (i, 0))
    fixed = lambda shape: pl.BlockSpec(shape, lambda i: (0,) * len(shape))
    return pl.pallas_call(
        lambda *refs: attend_back_kernel(heads, size, *refs),
        grid=(tokens // length,),
        in_specs=[
            by_block(width),
            fixed(w_out.shape),
            by_block(3 * heads * LANES),
            by_block(LANES),
            by_block(LANES),
            by_block(LANES),
            pl.BlockSpec((1, 1, length), lambda i: (i, 0, 0)),
            by_block(1),
            fixed(weight.shape),
            by_block(width),
        ],
        out_specs=[
            by_block(3 * part),
            by_block(width),
            fixed((1, 3 * part)),
            fixed((1, width)),
            fixed((1, width)),
        ],
        out_shape=[
            jax.ShapeDtypeStruct((tokens, 3 * part), BF16),
            jax.ShapeDtypeStruct((tokens, width), BF16),
            jax.ShapeDtypeStruct((1, 3 * part), F32),
            jax.ShapeDtypeStruct((1, width), F32),
            jax.ShapeDtypeStruct((1, width), F32),
        ],
        compiler_params=pltpu.CompilerParams(vmem_limit_bytes=48 * 1024 * 1024),
        cost_estimate=pl.CostEstimate(
            flops=2 * tokens * width * 4 * part + 10 * tokens * length * part,
            bytes_accessed=6 * tokens * width + weight.size * 2 + tokens * 3 * heads * LANES * 2,
            transcendentals=tokens * length * heads,
        ),
    )(db, w_out, qkv, lse, cosine, sine, seg_rows, seg_cols, weight, x)


def rotary(rows, columns, size):
    quarter = size // 4
    inverse = 10000.0 ** (-4.0 * jnp.arange(quarter, dtype=F32) / size)
    angles = jnp.concatenate(
        [rows.astype(F32)[:, None] * inverse, columns.astype(F32)[:, None] * inverse], -1
    )
    cosine, sine = jnp.cos(angles), jnp.sin(angles)
    nothing = jnp.zeros((rows.shape[0], LANES - size), F32)
    return (
        jnp.concatenate([cosine, cosine, nothing], -1),
        jnp.concatenate([-sine, sine, nothing], -1),
    )


def on_device(
    shards,
    hidden_in,
    seg_ids,
    patch_rows,
    patch_cols,
    ln1_scale,
    ln1_shift,
    qkv_weight,
    qkv_bias,
    out_weight,
    out_bias,
    ln2_scale,
    ln2_shift,
    up_weight,
    up_bias,
    down_weight,
    down_bias,
    cotangent,
):
    copies = 4
    me = lax.axis_index("rep")
    length, width = hidden_in.shape
    rows = ln1_scale.shape[0]
    size = width // HEADS
    heads = HEADS // copies
    part = heads * size
    hidden = up_weight.shape[1]
    own_hidden = hidden // copies
    step = hidden // shards // copies

    def own(array, axis):
        return lax.dynamic_index_in_dim(array, me, axis, False)

    own_qkv = own(qkv_weight.reshape(rows, 3, copies, part), 2).reshape(rows, 3 * part)
    own_up = own(up_weight.reshape(rows, shards, copies, step), 2).reshape(rows, own_hidden)
    own_down = own(down_weight.reshape(copies, step, width), 0)
    own_out = own(out_weight.reshape(copies, rows // copies, width), 0)
    vectors = (
        ln1_scale, ln1_shift, out_bias, ln2_scale, ln2_shift, down_bias, qkv_bias, up_bias,
    )
    small = jnp.concatenate(vectors)
    small_rows = 8
    small = jnp.pad(small, (0, small_rows * 3 * part - small.size)).reshape(small_rows, 3 * part)
    first, up_full, out_all, down_full = gather_shards(
        [
            jnp.concatenate([own_qkv, small]),
            own_up,
            own_out,
            own_down,
        ],
        shards,
    )
    w_qkv = first[:, :rows].reshape(width, 3 * part)
    small = first[:, rows:].reshape(shards, -1)
    up_full = up_full.reshape(width, own_hidden)
    down_full = down_full.reshape(own_hidden, width)
    full = []
    at = 0
    for vector in vectors:
        full.append(small[:, at : at + vector.size].astype(F32))
        at += vector.size
    gain_one, shift_one, out_offset, gain_two, shift_two, down_offset = (
        v.reshape(1, width) for v in full[:6]
    )
    qkv_offset = own(full[6].reshape(3, copies, part), 1).reshape(1, 3 * part)
    up_offset = own(full[7].reshape(shards, copies, step), 1).reshape(1, own_hidden)

    ids = jnp.concatenate([seg_ids, patch_rows, patch_cols])
    ids = jnp.stack(gather_rep(ids))
    seg_rows, seg_cols = ids[:, :1], ids[:, 0].reshape(-1, 1)
    x_low = jnp.concatenate(gather_rep(hidden_in))
    grad_out = jnp.concatenate(gather_rep(cotangent))
    tokens = x_low.shape[0]
    cosine, sine = rotary(ids[:, 1].reshape(-1), ids[:, 2].reshape(-1), size)

    normed_one, qkv, lse, mixed = attend(
        x_low, gain_one, shift_one, w_qkv, qkv_offset, cosine, sine, seg_rows, seg_cols, heads, size
    )
    out_full = jnp.stack(by_owner(gather_rep(out_all), me), 1).reshape(width, width)
    blocks = mixed.reshape(copies, length, part)
    near, far = to_core(blocks), to_x(blocks)
    both = to_core(far)
    mixed_slots = [
        mixed,
        near[jnp.array([1, 0, 3, 2])].reshape(tokens, part),
        far[jnp.array([2, 3, 0, 1])].reshape(tokens, part),
        both[jnp.array([3, 2, 1, 0])].reshape(tokens, part),
    ]
    mixed_full = jnp.concatenate(by_owner(mixed_slots, me), 1)

    middle = x_low.astype(F32) + times(mixed_full, out_full) + out_offset
    unit_two, inverse_two = norm_parts(middle)
    normed_two = (unit_two * gain_two + shift_two).astype(BF16)
    upward = times(normed_two, up_full) + up_offset
    sigma = jax.nn.sigmoid(GELU_SLOPE * upward)
    activated = (upward * sigma).astype(BF16)
    slope = sigma + GELU_SLOPE * upward * sigma * (1.0 - sigma)

    grad_down = outer(activated, grad_out).astype(BF16)
    grad_up_low = (times_transposed(grad_out, down_full) * slope).astype(BF16)
    grad_normed_two = sum_rep(times_transposed(grad_up_low, up_full).reshape(copies, length, width))
    grad_up = outer(normed_two, grad_up_low).astype(BF16)
    grad_up_bias = jnp.sum(grad_up_low.astype(F32), 0)
    branch = scatter_rep(times(activated, down_full).reshape(copies, length, width))
    output = middle[:length] + branch + down_offset

    grad_normed_two = grad_normed_two.reshape(tokens, width).astype(F32)
    grad_middle = grad_out.astype(F32) + norm_back(
        grad_normed_two, unit_two, inverse_two, gain_two
    )
    grad_branch = grad_middle.astype(BF16)
    grad_out_w = outer(mixed_full, own(grad_branch.reshape(tokens, copies, part), 1)).astype(BF16)

    own_w_out = lax.dynamic_slice_in_dim(out_full, me * part, part, 0)
    grad_qkv_low, grad_normed_one, sum_qkv, sum_gain, sum_shift = attend_back(
        grad_branch, own_w_out, qkv, lse, cosine, sine, seg_rows, seg_cols, w_qkv, x_low, heads, size
    )
    grad_qkv = outer(normed_one, grad_qkv_low).astype(BF16)
    grad_normed_one = scatter_rep(grad_normed_one.reshape(copies, length, width))
    unit_one, inverse_one = norm_parts(hidden_in.astype(F32))
    grad_inputs = grad_middle[:length] + norm_back(grad_normed_one, unit_one, inverse_one, gain_one)

    def sum_of(values):
        return jnp.sum(values[:length], 0).reshape(shards, rows)

    def placed(values, like, axis):
        return lax.dynamic_update_index_in_dim(jnp.zeros(like, F32), values, me, axis)

    sums = [
        sum_gain.reshape(shards, rows),
        sum_shift.reshape(shards, rows),
        sum_of(grad_branch.astype(F32)),
        sum_of(grad_normed_two * unit_two),
        sum_of(grad_normed_two),
        sum_of(grad_out.astype(F32)),
        placed(sum_qkv.reshape(3, part), (3, copies, part), 1).reshape(shards, -1),
        placed(grad_up_bias.reshape(shards, step), (shards, copies, step), 1).reshape(shards, -1),
    ]
    sums = jnp.concatenate(sums, 1)
    sums = jnp.pad(sums, ((0, 0), (0, small_rows * 3 * part - sums.shape[1])))
    last = jnp.concatenate(
        [grad_qkv.reshape(shards, rows, 3 * part), sums.astype(BF16).reshape(shards, small_rows, -1)],
        1,
    )

    done_down = scatter_shards(grad_down.reshape(shards, step, width), shards, 4)
    done_up = scatter_shards(grad_up.reshape(shards, rows, own_hidden), shards, 3)
    done_out = scatter_shards(grad_out_w.reshape(shards, rows, part), shards, 4)
    done_last = scatter_shards(last, shards, 4)

    whole_down = jnp.concatenate(by_owner(gather_rep(done_down), me), 0).astype(F32)
    whole_up = jnp.stack(
        [p.reshape(rows, shards, step) for p in by_owner(gather_rep(done_up), me)], 2
    )
    whole_up = whole_up.reshape(rows, hidden).astype(F32)
    whole_out = jnp.concatenate(by_owner(gather_rep(done_out), me), 1).astype(F32)
    last_slots = gather_rep(done_last)
    whole_qkv = jnp.stack(
        [p[:rows].reshape(rows, 3, part) for p in by_owner(last_slots, me)], 2
    )
    whole_qkv = whole_qkv.reshape(rows, 3 * width).astype(F32)
    summed = sum(p[rows:].astype(F32) for p in by_owner(last_slots, me)).reshape(-1)
    totals = []
    at = 0
    for vector in vectors:
        totals.append(summed[at : at + vector.size])
        at += vector.size
    return (
        output.astype(BF16),
        grad_inputs.astype(BF16),
        totals[0],
        totals[1],
        whole_qkv,
        totals[6],
        whole_out,
        totals[2],
        totals[3],
        totals[4],
        whole_up,
        totals[7],
        whole_down,
        totals[5],
    )


def solution(mesh):
    shards = mesh.shape["shard"]
    tokens, vector, matrix = P(("rep", "shard"), None), P("shard"), P("shard", None)
    in_specs = (
        (tokens,) * 4
        + (vector, vector, matrix, vector, matrix, vector)
        + (vector, vector, matrix, vector, matrix, vector)
        + (tokens,)
    )
    out_specs = (
        (tokens, tokens)
        + (vector, vector, matrix, vector, matrix, vector)
        + (vector, vector, matrix, vector, matrix, vector)
    )
    return jax.shard_map(
        lambda *args: on_device(shards, *args),
        mesh=mesh,
        in_specs=in_specs,
        out_specs=out_specs,
        check_vma=False,
    )
```

time: 2520 us -> 636 us (0.25)
  waiting for transfers between devices: 2110 us -> 221 us
  starting transfers between devices: 0.44 us -> 77.8 us
  blocking collectives: 71.1 us -> 0 us
  matrix products: 122 us -> 54 us
  other arithmetic: 10.3 us -> 54.9 us
  Pallas kernels: 0 us -> 38.1 us
  local copies, waits for them, and re-layouts: 181 us -> 155 us
    reduce_scatter x4 -> x0, waiting for transfers between devices: 1280 us -> none  [the longest x1 419 us: on_device(): lax.psum_scatter(grad_up, 'shard', scatter_dimension=0, tiled=True)]
    all_gather x4 -> x0, waiting for transfers between devices: 462 us -> none  [the longest x1 180 us: on_device(): lax.all_gather(up_weight, 'shard', axis=0, tiled=True)]
    unnamed x14 -> x0, waiting for transfers between devices: 362 us -> none
    ppermute x0 -> x90, waiting for transfers between devices: none -> 221 us  [the longest x14 77.7 us: gather_shards(): right = lax.ppermute(right, 'shard', RIGHT)]
    concatenate x1 -> x8, local copies, waits for them, and re-layouts: 87.4 us -> 8.2 us  [the longest x1 5.92 us: on_device(): mixed_full = jnp.concatenate(by_owner(mixed_slots, me), 1)]
    ppermute x0 -> x90, starting transfers between devices: none -> 77.8 us  [the longest x14 20.5 us: gather_shards(): left = lax.ppermute(left, 'shard', LEFT)]
    unnamed x1 -> x0, blocking collectives: 40.5 us -> none
    pallas_call x0 -> x2, Pallas kernels: none -> 38.1 us  [the longest x1 19.7 us: attend_back(): pl.pallas_call(lambda *refs: attend_back_kernel(heads, size, *refs), grid...]
  transfers between devices with their start and end apart: 11 -> 90, of which waited for: 11 -> 38; matrix products, arithmetic and copies ran while one was open for 4% -> 28% of each run, Pallas kernels for 0% -> 6%
where the time goes in v1:
time: 636 us; the launch traced here: 625 us
  waiting for transfers between devices  221 us (35%)
  local copies, waits for them, and re-layouts  155 us (24%)
  starting transfers between devices  77.8 us (12%)
  other arithmetic  54.9 us (9%)
  matrix products  54 us (8%)
  Pallas kernels  38.1 us (6%)
  between operations  24.5 us (4%)
    ppermute x14, waiting for transfers between devices, gather_shards(): right = lax.ppermute(right, 'shard', RIGHT)  77.7 us
    ppermute x15, waiting for transfers between devices, scatter_shards(): lax.ppermute(term if right is None else plus(right, term), 'shard', RIGHT)  57.9 us
    ppermute x12, waiting for transfers between devices, to_x(): return lax.ppermute(value, 'rep', X_PAIRS)  49.3 us
    dot_general x3, matrix products, times(): return jnp.dot(left, right, preferred_element_type=F32)  20.9 us
    ppermute x14, starting transfers between devices, gather_shards(): left = lax.ppermute(left, 'shard', LEFT)  20.5 us
    dot_general x4, matrix products, outer(): lax.dot_general(left, right, (((0,), (0,)), ((), ())), preferred_element_...  20.1 us
    pallas_call x1, Pallas kernels, attend_back(): pl.pallas_call(lambda *refs: attend_back_kernel(heads, size, *refs), grid...  19.7 us
    ppermute x13, waiting for transfers between devices, scatter_shards(): lax.ppermute(term if left is None else plus(left, term), 'shard', LEFT)  18.4 us
  transfers between devices with their start and end apart: 90, of which 38 were waited for; matrix products, arithmetic and copies ran while one was open for 28% of the time, Pallas kernels for 6%

profile of v1, /device:TPU:0, one launch (start us, length us, event | category | flops | bytes accessed | tf_op | source)
XLA Modules:
  0.0 624.8 jit_solution(15930479063205870814)
XLA Ops:
  94.1 9.3 %collective-permute-done.3 = bf16[168,960]{1,0:T(8,128)(2,1)S(1)} collective-permute-done((bf16[168,960]{1,0:T(8,128)(2,1)}, bf16[168,960]{1,0:T(8,128)(2,1)S(1)}, u32[]{:S(2)}, u32[]{:S(2)}) %collective-permute-start.3) | collective-permute-done | bytes 322592 | tf_op jit(solution)/shard_map/ppermute | solution.py:113
  107.0 6.8 %collective-permute-done.26 = bf16[160,1280]{1,0:T(8,128)(2,1)S(1)} collective-permute-done((bf16[160,1280]{1,0:T(8,128)(2,1)}, bf16[160,1280]{1,0:T(8,128)(2,1)S(1)}, u32[]{:S(2)}, u32[]{:S(2)}) %collective-permute-start.26) | collective-permute-done | bytes 409632 | tf_op jit(solution)/shard_map/ppermute | solution.py:113
  117.3 9.5 %collective-permute-done.33 = bf16[160,1280]{1,0:T(8,128)(2,1)S(1)} collective-permute-done((bf16[160,1280]{1,0:T(8,128)(2,1)S(1)}, bf16[160,1280]{1,0:T(8,128)(2,1)S(1)}, u32[]{:S(2)}, u32[]{:S(2)}) %collective-permute-start.33) | collective-permute-done | bytes 409632 | tf_op jit(solution)/shard_map/ppermute | solution.py:113
  132.6 6.6 %collective-permute-done.5 = bf16[168,960]{1,0:T(8,128)(2,1)S(1)} collective-permute-done((bf16[168,960]{1,0:T(8,128)(2,1)S(1)}, bf16[168,960]{1,0:T(8,128)(2,1)S(1)}, u32[]{:S(2)}, u32[]{:S(2)}) %collective-permute-start.5) | collective-permute-done | bytes 322592 | tf_op jit(solution)/shard_map/ppermute | solution.py:113
  162.1 6.4 %collective-permute-done.35 = bf16[160,1280]{1,0:T(8,128)(2,1)S(1)} collective-permute-done((bf16[160,1280]{1,0:T(8,128)(2,1)S(1)}, bf16[160,1280]{1,0:T(8,128)(2,1)S(1)}, u32[]{:S(2)}, u32[]{:S(2)}) %collective-permute-start.35) | collective-permute-done | bytes 409632 | tf_op jit(solution)/shard_map/ppermute | solution.py:113
  170.7 6.1 collective-permute-done.7
  178.9 6.1 collective-permute-done.30
  186.7 6.4 %collective-permute-done.31 = bf16[160,1280]{1,0:T(8,128)(2,1)} collective-permute-done((bf16[160,1280]{1,0:T(8,128)(2,1)S(1)}, bf16[160,1280]{1,0:T(8,128)(2,1)}, u32[]{:S(2)}, u32[]{:S(2)}) %collective-permute-start.31) | collective-permute-done | bytes 409632 | tf_op jit(solution)/shard_map/ppermute | solution.py:118
  202.7 6.4 %collective-permute-done.38 = bf16[160,1280]{1,0:T(8,128)(2,1)} collective-permute-done((bf16[160,1280]{1,0:T(8,128)(2,1)S(1)}, bf16[160,1280]{1,0:T(8,128)(2,1)}, u32[]{:S(2)}, u32[]{:S(2)}) %collective-permute-start.38) | collective-permute-done | bytes 409632 | tf_op jit(solution)/shard_map/ppermute | solution.py:118
  228.5 18.4 %shard_map.920 = (bf16[1024,1280]{1,0:T(8,128)(2,1)S(1)}, bf16[1024,1536]{1,0:T(8,128)(2,1)}, f32[1024,128]{1,0:T(8,128)S(1)}, bf16[1024,320]{1,0:T(8,128)(2,1)S(1)}) custom-call(bf16[1024,1280]{1,0:T(8,128)(2,1)} %constant_dynamic-update-slice_fusion.refs_0_.refs_9_, f32[1,1280]{1,0:T(1,128)S(1)} %reshape.314.refs_1_, f32[1,1280]{1,0:T(1,128)S(1)} %reshape.348.refs_2_, ...), custom_call_target="tpu_custom_call" | custom-call | flops 2852126720 | bytes 10846208 | tf_op jit(solution)/shard_map/pallas_call | solution.py:204
  259.9 7.1 %collective-permute-done.13 = bf16[4,256,320]{1,2,0:T(8,128)(2,1)} collective-permute-done((bf16[4,256,320]{1,2,0:T(8,128)(2,1)}, bf16[4,256,320]{1,2,0:T(8,128)(2,1)}, u32[]{:S(2)}, u32[]{:S(2)}) %collective-permute-start.13) | collective-permute-done | bytes 655392 | tf_op jit(solution)/shard_map/ppermute | solution.py:58
  287.0 5.9 concatenate.47
  292.9 7.3 %fusion.59 = (f32[1024]{0:T(1024)S(1)}, f32[1024,1280]{1,0:T(8,128)S(1)}) fusion(f32[1280]{0:T(1024)S(1)} %reshape.351, bf16[1024,1280]{1,0:T(8,128)(2,1)} %constant_dynamic-update-slice_fusion.refs_0_.refs_9_, bf16[1024,1280]{1,0:T(8,128)(2,1)} %concatenate.47, bf16[1280,1280]{1,0:T(8,128)(2,1)} %bitcast.287), kind=kOutput, calls=%fused_computation.285 | convolution fusion | flops 3360685056 | bytes 13771776 | tf_op jit(solution)/shard_map/dot_general | solution.py:50
  303.1 8.0 %multiply_convert_fusion.1 = (bf16[1024,1280]{1,0:T(8,128)(2,1)S(1)}, f32[1024,1280]{1,0:T(8,128)S(1)}) fusion(f32[1280]{0:T(1024)S(1)} %add.927, bf16[1280,1280]{1,0:T(8,128)(2,1)} %bitcast.53, f32[1024,1280]{1,0:T(8,128)S(1)} %subtract_multiply_fusion, f32[1280]{0:T(1024)S(1)} %reshape.353, f32[1280]{0:T(1024)S(1)} %reshape.352), kind=kOutput, calls=%fused_computation.18 | convolution fusion | flops 3368550400 | bytes 16399360 | tf_op jit(solution)/shard_map/dot_general | solution.py:50
  323.4 7.2 %convert_reduce_fusion = (bf16[1280]{0:T(1024)(128)(2,1)S(1)}, bf16[1024,1280]{1,0:T(8,128)(2,1)S(1)}) fusion(f32[1024,1280]{1,0:T(8,128)S(1)} %get-tuple-element.139, f32[1280]{0:T(1024)S(1)} %add.927, bf16[1024,1280]{1,0:T(8,128)(2,1)S(1)} %copy-done.9, bf16[1280,1280]{1,0:T(8,128)(2,1)} %bitcast.64), kind=kOutput, calls=%fused_computation.13 | convolution fusion | flops 3372481280 | bytes 13770240 | tf_op jit(solution)/shard_map/dot_general | solution.py:46
  358.4 10.7 %collective-permute-done.80 = bf16[160,1280]{1,0:T(8,128)(2,1)S(1)} collective-permute-done((bf16[160,1280]{1,0:T(8,128)(2,1)S(1)}, bf16[160,1280]{1,0:T(8,128)(2,1)S(1)}, u32[]{:S(2)}, u32[]{:S(2)}) %collective-permute-start.80) | collective-permute-done | bytes 409632 | tf_op jit(solution)/shard_map/ppermute | solution.py:141
  371.3 8.9 %collective-permute-done.74 = bf16[160,1280]{1,0:T(8,128)(2,1)S(1)} collective-permute-done((bf16[160,1280]{1,0:T(8,128)(2,1)S(1)}, bf16[160,1280]{1,0:T(8,128)(2,1)S(1)}, u32[]{:S(2)}, u32[]{:S(2)}) %collective-permute-start.74) | collective-permute-done | bytes 409632 | tf_op jit(solution)/shard_map/ppermute | solution.py:144
  384.7 8.2 %collective-permute-done.71 = bf16[160,1280]{1,0:T(8,128)(2,1)S(1)} collective-permute-done((bf16[160,1280]{1,0:T(8,128)(2,1)S(1)}, bf16[160,1280]{1,0:T(8,128)(2,1)S(1)}, u32[]{:S(2)}, u32[]{:S(2)}) %collective-permute-start.71) | collective-permute-done | bytes 409632 | tf_op jit(solution)/shard_map/ppermute | solution.py:141
  395.2 6.5 %collective-permute-done.82 = bf16[160,1280]{1,0:T(8,128)(2,1)S(1)} collective-permute-done((bf16[160,1280]{1,0:T(8,128)(2,1)S(1)}, bf16[160,1280]{1,0:T(8,128)(2,1)S(1)}, u32[]{:S(2)}, u32[]{:S(2)}) %collective-permute-start.82) | collective-permute-done | bytes 409632 | tf_op jit(solution)/shard_map/ppermute | solution.py:141
  419.7 37.6 %collective-permute-done.77 = bf16[160,1280]{1,0:T(8,128)(2,1)S(1)} collective-permute-done((bf16[160,1280]{1,0:T(8,128)(2,1)S(1)}, bf16[160,1280]{1,0:T(8,128)(2,1)S(1)}, u32[]{:S(2)}, u32[]{:S(2)}) %collective-permute-start.77) | collective-permute-done | bytes 409632 | tf_op jit(solution)/shard_map/ppermute | solution.py:58
  484.7 19.7 %shard_map.921 = (bf16[1024,960]{1,0:T(8,128)(2,1)S(1)}, bf16[1024,1280]{1,0:T(8,128)(2,1)}, f32[1,960]{1,0:T(1,128)S(1)}, f32[1,1280]{1,0:T(1,128)S(1)}, f32[1,1280]{1,0:T(1,128)S(1)}) custom-call(bf16[1024,1280]{1,0:T(8,128)(2,1)} %get-tuple-element.34.refs_0_, bf16[320,1280]{1,0:T(8,128)(2,1)S(1)} %constant_dynamic-slice_fusion.refs_1_, ...), custom_call_target="tpu_custom_call" | custom-call | flops 4194304000 | bytes 13467648 | tf_op jit(solution)/shard_map/pallas_call | solution.py:290
  514.0 5.9 convolution_convert_fusion.4
  532.1 7.9 %collective-permute-done.61 = bf16[160,320]{1,0:T(8,128)(2,1)S(1)} collective-permute-done((bf16[160,320]{1,0:T(8,128)(2,1)S(1)}, bf16[160,320]{1,0:T(8,128)(2,1)S(1)}, u32[]{:S(2)}, u32[]{:S(2)}) %collective-permute-start.61) | collective-permute-done | bytes 102432 | tf_op jit(solution)/shard_map/ppermute | solution.py:141
  600.7 7.9 %reshape.378 = f32[160,5120]{1,0:T(8,128)} reshape(f32[160,8,4,160]{3,2,1,0:T(4,128)} %copy.207) | data formatting | bytes 6553600 | tf_op jit(solution)/shard_map/convert_element_type | solution.py:497
  (490 shorter events, 369.8 us)
Async XLA Ops:
  1.6 62.7 %collective-permute-start.10 = (s32[3,256]{1,0:T(4,128)S(1)}, s32[3,256]{1,0:T(4,128)S(1)}, u32[]{:S(2)}, u32[]{:S(2)}) collective-permute-start(s32[3,256]{1,0:T(4,128)S(1)} %get-tuple-element.125), channel_id=1, source_target_pairs={{0,8},{8,0},{16,24},{24,16},{1,9},{9,1},{17,25},{25,17},{2,10},{10... | collective-permute-start | bytes 9224 | tf_op jit(solution)/shard_map/ppermute | solution.py:54
  2.0 47.1 %collective-permute-start.11 = (s32[3,256]{1,0:T(4,128)S(1)}, s32[3,256]{1,0:T(4,128)S(1)}, u32[]{:S(2)}, u32[]{:S(2)}) collective-permute-start(s32[3,256]{1,0:T(4,128)S(1)} %get-tuple-element.125), channel_id=1, source_target_pairs={{0,16},{16,0},{8,24},{24,8},{1,17},{17,1},{9,25},{25,9},{2,18},{18... | collective-permute-start | bytes 9224 | tf_op jit(solution)/shard_map/ppermute | solution.py:58
  4.6 136.6 %collective-permute-start.42 = (bf16[256,1280]{1,0:T(8,128)(2,1)}, bf16[256,1280]{1,0:T(8,128)(2,1)}, u32[]{:S(2)}, u32[]{:S(2)}) collective-permute-start(bf16[256,1280]{1,0:T(8,128)(2,1)} %param.105), channel_id=1, source_target_pairs={{0,8},{8,0},{16,24},{24,16},{1,9},{9,1},{17,25},{25,17},{2,10},{10... | collective-permute-start | bytes 1966088 | tf_op jit(solution)/shard_map/ppermute | solution.py:54
  4.7 139.0 %collective-permute-start.43 = (bf16[256,1280]{1,0:T(8,128)(2,1)}, bf16[256,1280]{1,0:T(8,128)(2,1)}, u32[]{:S(2)}, u32[]{:S(2)}) collective-permute-start(bf16[256,1280]{1,0:T(8,128)(2,1)} %param.105), channel_id=1, source_target_pairs={{0,16},{16,0},{8,24},{24,8},{1,17},{17,1},{9,25},{25,9},{2,18},{18... | collective-permute-start | bytes 1966088 | tf_op jit(solution)/shard_map/ppermute | solution.py:58
  5.0 143.6 %collective-permute-start.1 = (bf16[256,1280]{1,0:T(8,128)(2,1)}, bf16[256,1280]{1,0:T(8,128)(2,1)}, u32[]{:S(2)}, u32[]{:S(2)}) collective-permute-start(bf16[256,1280]{1,0:T(8,128)(2,1)} %param.89), channel_id=1, source_target_pairs={{0,16},{16,0},{8,24},{24,8},{1,17},{17,1},{9,25},{25,9},{2,18},{18... | collective-permute-start | bytes 1966088 | tf_op jit(solution)/shard_map/ppermute | solution.py:58
  70.9 33.7 %collective-permute-start.4 = (bf16[168,960]{1,0:T(8,128)(2,1)}, bf16[168,960]{1,0:T(8,128)(2,1)S(1)}, u32[]{:S(2)}, u32[]{:S(2)}) collective-permute-start(bf16[168,960]{1,0:T(8,128)(2,1)} %copy-done.27), channel_id=1, source_target_pairs={{0,1},{2,0},{4,2},{6,4},{7,6},{5,7},{3,5},{1,3},{8,9},{10,8},{12,1... | collective-permute-start | bytes 967688 | tf_op jit(solution)/shard_map/ppermute | solution.py:118
  139.9 129.6 %collective-permute-start.25 = (bf16[8,40,1280]{2,1,0:T(8,128)(2,1)}, bf16[8,40,1280]{2,1,0:T(8,128)(2,1)}, u32[]{:S(2)}, u32[]{:S(2)}) collective-permute-start(bf16[8,40,1280]{2,1,0:T(8,128)(2,1)} %bitcast_dynamic-update-slice_fusion.22), channel_id=1, source_target_pairs={{0,8},{8,0},{16,24},{24,16},{1,9},{9,1},{17,25},{25,17},{2,10},{10... | collective-permute-start | bytes 2457608 | tf_op jit(solution)/shard_map/ppermute | solution.py:54
  141.2 83.1 %collective-permute-start.23 = (bf16[8,40,1280]{2,1,0:T(8,128)(2,1)}, bf16[8,40,1280]{2,1,0:T(8,128)(2,1)}, u32[]{:S(2)}, u32[]{:S(2)}) collective-permute-start(bf16[8,40,1280]{2,1,0:T(8,128)(2,1)} %bitcast_dynamic-update-slice_fusion.22), channel_id=1, source_target_pairs={{0,16},{16,0},{8,24},{24,8},{1,17},{17,1},{9,25},{25,9},{2,18},{18... | collective-permute-start | bytes 2457608 | tf_op jit(solution)/shard_map/ppermute | solution.py:58
  169.9 54.4 %collective-permute-start.44 = (bf16[256,1280]{1,0:T(8,128)(2,1)}, bf16[256,1280]{1,0:T(8,128)(2,1)S(1)}, u32[]{:S(2)}, u32[]{:S(2)}) collective-permute-start(bf16[256,1280]{1,0:T(8,128)(2,1)} %collective-permute-done.43), channel_id=1, source_target_pairs={{0,8},{8,0},{16,24},{24,16},{1,9},{9,1},{17,25},{25,17},{2,10},{10... | collective-permute-start | bytes 1966088 | tf_op jit(solution)/shard_map/ppermute | solution.py:54
  178.1 49.5 %collective-permute-start.2 = (bf16[256,1280]{1,0:T(8,128)(2,1)}, bf16[256,1280]{1,0:T(8,128)(2,1)S(1)}, u32[]{:S(2)}, u32[]{:S(2)}) collective-permute-start(bf16[256,1280]{1,0:T(8,128)(2,1)} %collective-permute-done.1), channel_id=1, source_target_pairs={{0,8},{8,0},{16,24},{24,16},{1,9},{9,1},{17,25},{25,17},{2,10},{10... | collective-permute-start | bytes 1966088 | tf_op jit(solution)/shard_map/ppermute | solution.py:54
  216.3 33.8 %collective-permute-start.32 = (bf16[160,1280]{1,0:T(8,128)(2,1)}, bf16[160,1280]{1,0:T(8,128)(2,1)}, u32[]{:S(2)}, u32[]{:S(2)}) collective-permute-start(bf16[160,1280]{1,0:T(8,128)(2,1)} %collective-permute-done.31), channel_id=1, source_target_pairs={{0,1},{2,0},{4,2},{6,4},{7,6},{5,7},{3,5},{1,3},{8,9},{10,8},{12,1... | collective-permute-start | bytes 1228808 | tf_op jit(solution)/shard_map/ppermute | solution.py:118
  224.3 29.1 %collective-permute-start.39 = (bf16[160,1280]{1,0:T(8,128)(2,1)}, bf16[160,1280]{1,0:T(8,128)(2,1)}, u32[]{:S(2)}, u32[]{:S(2)}) collective-permute-start(bf16[160,1280]{1,0:T(8,128)(2,1)} %collective-permute-done.38), channel_id=1, source_target_pairs={{0,1},{2,0},{4,2},{6,4},{7,6},{5,7},{3,5},{1,3},{8,9},{10,8},{12,1... | collective-permute-start | bytes 1228808 | tf_op jit(solution)/shard_map/ppermute | solution.py:118
  224.3 45.2 %collective-permute-start.24 = (bf16[8,40,1280]{2,1,0:T(8,128)(2,1)}, bf16[8,40,1280]{2,1,0:T(8,128)(2,1)}, u32[]{:S(2)}, u32[]{:S(2)}) collective-permute-start(bf16[8,40,1280]{2,1,0:T(8,128)(2,1)} %collective-permute-done.23), channel_id=1, source_target_pairs={{0,8},{8,0},{16,24},{24,16},{1,9},{9,1},{17,25},{25,17},{2,10},{10... | collective-permute-start | bytes 2457608 | tf_op jit(solution)/shard_map/ppermute | solution.py:54
  344.6 61.0 %collective-permute-start.40 = (bf16[2,256,1280]{2,1,0:T(8,128)(2,1)S(1)}, bf16[2,256,1280]{2,1,0:T(8,128)(2,1)S(1)}, u32[]{:S(2)}, u32[]{:S(2)}) collective-permute-start(bf16[2,256,1280]{2,1,0:T(8,128)(2,1)S(1)} %pad_maximum_fusion.1), channel_id=1, source_target_pairs={{0,8},{8,0},{16,24},{24,16},{1,9},{9,1},{17,25},{25,17},{2,10},{10... | collective-permute-start | bytes 3932168 | tf_op jit(solution)/shard_map/ppermute | solution.py:54
  348.4 55.6 %collective-permute-start.45 = (bf16[2,256,1280]{2,1,0:T(8,128)(2,1)S(1)}, bf16[2,256,1280]{2,1,0:T(8,128)(2,1)S(1)}, u32[]{:S(2)}, u32[]{:S(2)}) collective-permute-start(bf16[2,256,1280]{2,1,0:T(8,128)(2,1)S(1)} %pad_maximum_fusion.2), channel_id=1, source_target_pairs={{0,8},{8,0},{16,24},{24,16},{1,9},{9,1},{17,25},{25,17},{2,10},{10... | collective-permute-start | bytes 3932168 | tf_op jit(solution)/shard_map/ppermute | solution.py:54
  405.7 53.1 %collective-permute-start.46 = (bf16[2,256,1280]{2,1,0:T(8,128)(2,1)S(1)}, bf16[2,256,1280]{2,1,0:T(8,128)(2,1)S(1)}, u32[]{:S(2)}, u32[]{:S(2)}) collective-permute-start(bf16[2,256,1280]{2,1,0:T(8,128)(2,1)S(1)} %add_convert_fusion.3), channel_id=1, source_target_pairs={{0,16},{16,0},{8,24},{24,8},{1,17},{17,1},{9,25},{25,9},{2,18},{18... | collective-permute-start | bytes 3932168 | tf_op jit(solution)/shard_map/ppermute | solution.py:58
  410.4 48.9 %collective-permute-start.41 = (bf16[256,1280]{1,0:T(8,128)(2,1)S(1)}, bf16[256,1280]{1,0:T(8,128)(2,1)S(1)}, u32[]{:S(2)}, u32[]{:S(2)}) collective-permute-start(bf16[256,1280]{1,0:T(8,128)(2,1)S(1)} %slice_bitcast_fusion.2), channel_id=1, source_target_pairs={{0,16},{16,0},{8,24},{24,8},{1,17},{17,1},{9,25},{25,9},{2,18},{18... | collective-permute-start | bytes 1966088 | tf_op jit(solution)/shard_map/ppermute | solution.py:58
  414.2 51.4 %collective-permute-start.79 = (bf16[160,1280]{1,0:T(8,128)(2,1)S(1)}, bf16[160,1280]{1,0:T(8,128)(2,1)S(1)}, u32[]{:S(2)}, u32[]{:S(2)}) collective-permute-start(bf16[160,1280]{1,0:T(8,128)(2,1)S(1)} %fusion.21), channel_id=1, source_target_pairs={{0,8},{8,0},{16,24},{24,16},{1,9},{9,1},{17,25},{25,17},{2,10},{10... | collective-permute-start | bytes 1228808 | tf_op jit(solution)/shard_map/ppermute | solution.py:54
  416.9 40.4 %collective-permute-start.77 = (bf16[160,1280]{1,0:T(8,128)(2,1)S(1)}, bf16[160,1280]{1,0:T(8,128)(2,1)S(1)}, u32[]{:S(2)}, u32[]{:S(2)}) collective-permute-start(bf16[160,1280]{1,0:T(8,128)(2,1)S(1)} %fusion.21), channel_id=1, source_target_pairs={{0,16},{16,0},{8,24},{24,8},{1,17},{17,1},{9,25},{25,9},{2,18},{18... | collective-permute-start | bytes 1228808 | tf_op jit(solution)/shard_map/ppermute | solution.py:58
  419.7 133.5 %collective-permute-start.89 = (bf16[160,1280]{1,0:T(8,128)(2,1)}, bf16[160,1280]{1,0:T(8,128)(2,1)}, u32[]{:S(2)}, u32[]{:S(2)}) collective-permute-start(bf16[160,1280]{1,0:T(8,128)(2,1)} %fusion.15), channel_id=1, source_target_pairs={{0,8},{8,0},{16,24},{24,16},{1,9},{9,1},{17,25},{25,17},{2,10},{10... | collective-permute-start | bytes 1228808 | tf_op jit(solution)/shard_map/ppermute | solution.py:54
  465.6 89.1 %collective-permute-start.88 = (bf16[160,1280]{1,0:T(8,128)(2,1)}, bf16[160,1280]{1,0:T(8,128)(2,1)}, u32[]{:S(2)}, u32[]{:S(2)}) collective-permute-start(bf16[160,1280]{1,0:T(8,128)(2,1)} %collective-permute-done.87), channel_id=1, source_target_pairs={{0,8},{8,0},{16,24},{24,16},{1,9},{9,1},{17,25},{25,17},{2,10},{10... | collective-permute-start | bytes 1228808 | tf_op jit(solution)/shard_map/ppermute | solution.py:54
  547.6 35.8 %collective-permute-start.48 = (bf16[2,256,1280]{2,1,0:T(8,128)(2,1)}, bf16[2,256,1280]{2,1,0:T(8,128)(2,1)}, u32[]{:S(2)}, u32[]{:S(2)}) collective-permute-start(bf16[2,256,1280]{2,1,0:T(8,128)(2,1)} %pad_maximum_fusion.3), channel_id=1, source_target_pairs={{0,8},{8,0},{16,24},{24,16},{1,9},{9,1},{17,25},{25,17},{2,10},{10... | collective-permute-start | bytes 3932168 | tf_op jit(solution)/shard_map/ppermute | solution.py:54
  579.8 28.8 %collective-permute-start.69 = (bf16[160,320]{1,0:T(8,128)(2,1)S(1)}, bf16[160,320]{1,0:T(8,128)(2,1)}, u32[]{:S(2)}, u32[]{:S(2)}) collective-permute-start(bf16[160,320]{1,0:T(8,128)(2,1)S(1)} %fusion.46), channel_id=1, source_target_pairs={{0,8},{8,0},{16,24},{24,16},{1,9},{9,1},{17,25},{25,17},{2,10},{10... | collective-permute-start | bytes 307208 | tf_op jit(solution)/shard_map/ppermute | solution.py:54
  579.8 28.8 %collective-permute-start.68 = (bf16[160,320]{1,0:T(8,128)(2,1)}, bf16[160,320]{1,0:T(8,128)(2,1)}, u32[]{:S(2)}, u32[]{:S(2)}) collective-permute-start(bf16[160,320]{1,0:T(8,128)(2,1)} %collective-permute-done.67), channel_id=1, source_target_pairs={{0,8},{8,0},{16,24},{24,16},{1,9},{9,1},{17,25},{25,17},{2,10},{10... | collective-permute-start | bytes 307208 | tf_op jit(solution)/shard_map/ppermute | solution.py:54
  (115 other events, 1372.7 us)
